TPU v7x, 32 devices: a whole 2x2x4 slice. The times are simulated.
32 devices in a mesh: member: 2 (over x), patch: 16 (over z, y, core).
Axes of the slice: x: 2, y: 2, z: 4, core: 2. Of those that a mesh axis runs over, the one named last changes fastest.
Arguments:
- log_rate: float32 [65536, 128], P(('member', 'patch')), parts along dimension 0, may hold values from -3 to 3
- log_state: float32 [65536, 128], P(('member', 'patch')), parts along dimension 0, may hold values from -3 to 3
- near_blocks: bfloat16 [512, 12, 128, 128], P(('member', 'patch')), parts along dimension 0, may hold values from -0.15625 to 0.15625
- near_columns: int32 [512, 12], P(('member', 'patch')), parts along dimension 0, may hold values from 0 to 255, as said below
- far_basis: bfloat16 [8, 32, 32768], P('member', None, 'patch'), parts along dimension 0, may hold values from -0.0625 to 0.0625
- far_coupling: bfloat16 [8, 32, 32768], P('member', None, 'patch'), parts along dimension 0, may hold values from -0.5 to 0.5
- self_stiffness: float32 [65536], P(('member', 'patch')), parts along dimension 0, may hold values from 1 to 3
- plate_rate: float32 [65536], P(('member', 'patch')), parts along dimension 0, may hold values from 0.5 to 2
- direct_effect: float32 [65536], P(('member', 'patch')), parts along dimension 0, may hold values from 0.3 to 1
- evolution_effect: float32 [65536], P(('member', 'patch')), parts along dimension 0, may hold values from 0.5 to 1.5
- triangle_area: float32 [65536], P(('member', 'patch')), parts along dimension 0, may hold values from 0.5 to 10.5
Outputs:
- new_log_rate: float32 [65536, 128], P(('member', 'patch')), parts along dimension 0
- new_log_state: float32 [65536, 128], P(('member', 'patch')), parts along dimension 0
- error_norm: float32 [256], P('member'), parts along dimension 0
There are 2 independent parts, one for each index of `member`. A program takes and returns all parts, laid end to end along the dimension named above; each array names one. Nothing has to cross between parts.
Inputs may be any that keep to these rules, and one draw needn't show every extreme that they name: `near_columns`: row block r's 12 column blocks are distinct, each is (r + o) mod 256 with -6 <= o <= 6, and they include r itself and both blocks at distance 6.
All inputs are finite; a program needn't handle non-finite values.
Results may differ from a plain program's by a relative error of at most 0.0012.
Values may be sent and summed in bfloat16 or wider, within the bound.
A program may use at most 128 MiB of HBM per device.

v0:
```python
import jax
import jax.numpy as jnp
from jax import lax
from jax.sharding import PartitionSpec as P

REACH = 6


step_size = 0.1
damping = 0.5
error_scale = 0.01


def partner_2(value, axis, stride):
    mask = 2**stride
    pairs = [(source, source ^ mask) for source in range(lax.axis_size(axis))]
    return lax.ppermute(value, axis, pairs)


def padded(cells, sides, width):
    for axis, dim in sides:
        count = lax.axis_size(axis)
        head = lax.slice_in_dim(cells, 0, width, axis=dim)
        tail = lax.slice_in_dim(cells, cells.shape[dim] - width, cells.shape[dim], axis=dim)
        cells = jnp.concatenate(
            [
                lax.ppermute(tail, axis, [(i, (i + 1) % count) for i in range(count)]),
                cells,
                lax.ppermute(head, axis, [((i + 1) % count, i) for i in range(count)]),
            ],
            axis=dim,
        )
    return cells


def partner_sums(projected, levels):
    coupled = []
    current = projected
    for tree_level in range(levels):
        partner = partner_2(current, "patch", tree_level)
        coupled.append(partner[0])
        current = current[1:] + partner[1:]
    return jnp.stack(coupled)


def on_device(
    log_rate,
    log_state,
    near_blocks,
    near_columns,
    far_basis,
    far_coupling,
    self_stiffness,
    plate_rate,
    direct_effect,
    evolution_effect,
    triangle_area,
):
    row_count, col_count = log_rate.shape
    row_blocks, near_count, block_size, _ = near_blocks.shape
    devices = lax.axis_size("patch")
    levels = devices.bit_length() - 1
    total_blocks = devices * row_blocks
    halo_rows = REACH * block_size
    first_block = lax.axis_index("patch") * row_blocks
    local_index = jnp.arange(row_blocks, dtype=jnp.int32)
    offset = (
        near_columns - (first_block + local_index)[:, None] + total_blocks // 2
    ) % total_blocks - total_blocks // 2
    position = local_index[:, None] + REACH + offset
    basis_flat = far_basis.reshape(-1, row_count)
    coupling = far_coupling.reshape(-1, row_count)

    def section_rates(rate_now, state_now):
        velocity = jnp.exp(rate_now)
        rate_bf = velocity.astype(jnp.bfloat16)
        extended = padded(rate_bf, (("patch", 0),), halo_rows)
        column_blocks = extended.reshape(-1, block_size, col_count)
        chosen = column_blocks[position]
        near_term = jnp.einsum(
            "rkij,rkjb->rib", near_blocks, chosen, preferred_element_type=jnp.float32
        ).reshape(row_count, col_count)
        projected = jnp.dot(basis_flat, rate_bf, preferred_element_type=jnp.float32).reshape(
            levels, -1
        )
        coupled = partner_sums(projected, levels).reshape(-1, col_count).astype(jnp.bfloat16)
        far_term = lax.dot_general(
            coupling, coupled, (((0,), (0,)), ((), ())), preferred_element_type=jnp.float32
        )
        stress_rate = (
            self_stiffness[:, None] * (plate_rate[:, None] - velocity) - near_term - far_term
        )
        state_rate = jnp.exp(-state_now) - velocity
        log_rate_rate = (stress_rate - evolution_effect[:, None] * state_rate) / (
            direct_effect[:, None] + damping * velocity
        )
        return (log_rate_rate, state_rate)

    rate_one, state_one = section_rates(log_rate, log_state)
    rate_two, state_two = section_rates(
        log_rate + step_size * rate_one, log_state + step_size * state_one
    )
    half_step = 0.5 * step_size
    new_log_rate = log_rate + half_step * (rate_one + rate_two)
    new_log_state = log_state + half_step * (state_one + state_two)
    rate_error = half_step * (rate_two - rate_one) / error_scale
    state_error = half_step * (state_two - state_one) / error_scale
    area_terms = jnp.sum(
        triangle_area[:, None] * (rate_error * rate_error + state_error * state_error), axis=0
    )
    totals, area_total = lax.psum((area_terms, jnp.sum(triangle_area)), "patch")
    error_norm = jnp.sqrt(totals / area_total + 1e-06)
    return (new_log_rate, new_log_state, error_norm)


def solution(mesh):
    in_specs = (
        P(("member", "patch"), None),
        P(("member", "patch"), None),
        P(("member", "patch"), None, None, None),
        P(("member", "patch"), None),
        P("member", None, "patch"),
        P("member", None, "patch"),
        P(("member", "patch")),
        P(("member", "patch")),
        P(("member", "patch")),
        P(("member", "patch")),
        P(("member", "patch")),
    )
    out_specs = (P(("member", "patch"), None), P(("member", "patch"), None), P("member"))
    return jax.shard_map(
        on_device, mesh=mesh, in_specs=in_specs, out_specs=out_specs, check_vma=False
    )
```

profile of v0, /device:TPU:0, one launch (start us, length us, event | category | flops | bytes accessed | tf_op | source)
XLA Modules:
  0.0 121.0 jit_solution(16478524655796271360)
XLA Ops:
  0.6 0.0 copy-start
  0.6 1.6 %copy.34 = f32[2048,128]{0,1:T(8,128)S(1)} copy(f32[2048,128]{1,0:T(8,128)} %param.11) | data formatting | bytes 2097152 | tf_op args[0]
  2.3 0.1 exponential_convert_fusion
  2.4 1.3 %fusion.14 = f32[128,128]{1,0:T(8,128)S(1)} fusion(bf16[128,2048]{1,0:T(8,128)(2,1)} %bitcast.56, bf16[2048,128]{0,1:T(8,128)(2,1)S(1)} %exponential_convert_fusion), kind=kOutput, calls=%fused_computation.50 | convolution fusion | flops 67108864 | bytes 1114112 | tf_op jit(solution)/shard_map/dot_general | solution.py:83
  3.8 0.5 collective-permute-start.2
  4.4 5.7 %collective-permute-start.1 = (bf16[768,128]{0,1:T(8,128)(2,1)S(1)}, bf16[768,128]{0,1:T(8,128)(2,1)S(1)}, u32[]{:S(2)}, u32[]{:S(2)}) collective-permute-start(bf16[768,128]{0,1:T(8,128)(2,1)S(1)} %get-tuple-element.17), channel_id=1, source_target_pairs={{1,0},{2,1},{3,2},{4,3},{5,4},{6,5},{7,6},{8,7},{9,8},{10,9},{11,1... | collective-permute-start | bytes 589832 | tf_op jit(solution)/shard_map/ppermute | solution.py:29
  10.2 0.1 collective-permute-start.3
  10.2 4.2 %collective-permute-done.3 = f32[3,4096]{1,0:T(4,128)S(1)} collective-permute-done((f32[3,4096]{1,0:T(4,128)S(1)}, f32[3,4096]{1,0:T(4,128)S(1)}, u32[]{:S(2)}, u32[]{:S(2)}) %collective-permute-start.3) | collective-permute-done | bytes 49184 | tf_op jit(solution)/shard_map/ppermute | solution.py:17
  14.5 1.8 %collective-permute-start.4 = (f32[2,4096]{1,0:T(2,128)S(1)}, f32[2,4096]{1,0:T(2,128)S(1)}, u32[]{:S(2)}, u32[]{:S(2)}) collective-permute-start(f32[2,4096]{1,0:T(2,128)S(1)} %slice_add_fusion.3), channel_id=1, source_target_pairs={{0,4},{1,5},{2,6},{3,7},{4,0},{5,1},{6,2},{7,3},{8,12},{9,13},{10,... | collective-permute-start | bytes 98312 | tf_op jit(solution)/shard_map/ppermute | solution.py:17
  16.4 0.8 compare_select_fusion
  17.1 0.1 reshape.72
  17.2 1.3 %collective-permute-done.4 = f32[2,4096]{1,0:T(2,128)S(1)} collective-permute-done((f32[2,4096]{1,0:T(2,128)S(1)}, f32[2,4096]{1,0:T(2,128)S(1)}, u32[]{:S(2)}, u32[]{:S(2)}) %collective-permute-start.4) | collective-permute-done | bytes 32800 | tf_op jit(solution)/shard_map/ppermute | solution.py:17
  18.5 2.9 %collective-permute-start.5 = (bf16[1,4096]{1,0:T(2,128)(2,1)S(1)}, bf16[1,4096]{1,0:T(2,128)(2,1)S(1)}, u32[]{:S(2)}, u32[]{:S(2)}) collective-permute-start(bf16[1,4096]{1,0:T(2,128)(2,1)S(1)} %get-tuple-element.21), channel_id=1, source_target_pairs={{0,8},{1,9},{2,10},{3,11},{4,12},{5,13},{6,14},{7,15},{8,0},{9,1},... | collective-permute-start | bytes 24584 | tf_op jit(solution)/shard_map/ppermute | solution.py:17
  21.4 2.5 %copy.29 = f32[2048,128]{0,1:T(8,128)} copy(f32[2048,128]{1,0:T(8,128)} %param.12) | data formatting | bytes 2097152 | tf_op args[1]
  24.0 0.1 pad_maximum_fusion.2
  24.1 0.7 convert_element_type.27
  24.7 0.1 pad_maximum_fusion
  24.8 0.6 copy.27
  25.4 8.1 %gather_fusion = bf16[192,128,128]{2,1,0:T(8,128)(2,1)} fusion(bf16[28,128,128]{2,1,0:T(8,128)(2,1)S(1)} %bitcast.51, s32[1024]{0:T(1024)S(1)} %pad_clamp_fusion), kind=kCustom, calls=%fused_computation | custom fusion | bytes 12583680 | tf_op jit(solution)/shard_map/gather | solution.py:79
  33.5 6.4 %fusion.15 = f32[16,128,128,1]{1,2,3,0:T(8,128)S(1)} fusion(bf16[16,12,128,128]{3,2,1,0:T(8,128)(2,1)} %param.13, bf16[16,12,128,128]{3,2,1,0:T(8,128)(2,1)} %bitcast.53), kind=kOutput, calls=%fused_computation.51 | convolution fusion | flops 805306368 | bytes 13631488 | tf_op jit(solution)/shard_map/rkij,rkjb->rib/dot_general | solution.py:80
  40.0 1.3 %copy.28 = f32[2048,128]{0,1:T(8,128)} copy(f32[2048,128]{1,0:T(8,128)S(1)} %bitcast.54) | data formatting | bytes 2097152 | tf_op jit(solution)/shard_map/reshape | solution.py:82
  41.3 3.4 %fusion.9 = (bf16[2048,128]{0,1:T(8,128)(2,1)S(1)}, f32[2048,128]{0,1:T(8,128)}) fusion(f32[2048,128]{0,1:T(8,128)S(1)} %copy.34, f32[2048]{0:T(1024)S(1)} %copy-done.5, f32[2048,128]{0,1:T(8,128)} %copy.29, f32[2048]{0:T(1024)S(1)} %copy-done.7, bf16[128,128]{1,0:T(8,128)(2,1)S(1)} %copy-done.3, bf16[128,2048]{1,0:T(8,128)(2,1)S(1)} %bitcast.48, ...), kind=kOutput, calls=%fused_computation.45 | convolution fusion | flops 70778880 | bytes 5308416 | tf_op jit(solution)/shard_map/dot_general | solution.py:87
  44.7 0.3 convolution_bitcast_fusion.2
  45.0 0.1 collective-permute-start.8
  45.2 1.2 collective-permute-done.8
  46.4 0.7 collective-permute-start.9
  47.1 3.6 %collective-permute-done.9 = f32[3,4096]{1,0:T(4,128)S(1)} collective-permute-done((f32[3,4096]{1,0:T(4,128)S(1)}, f32[3,4096]{1,0:T(4,128)S(1)}, u32[]{:S(2)}, u32[]{:S(2)}) %collective-permute-start.9) | collective-permute-done | bytes 49184 | tf_op jit(solution)/shard_map/ppermute | solution.py:17
  50.8 1.6 %collective-permute-start.10 = (f32[2,4096]{1,0:T(2,128)S(1)}, f32[2,4096]{1,0:T(2,128)S(1)}, u32[]{:S(2)}, u32[]{:S(2)}) collective-permute-start(f32[2,4096]{1,0:T(2,128)S(1)} %slice_add_fusion.2), channel_id=1, source_target_pairs={{0,4},{1,5},{2,6},{3,7},{4,0},{5,1},{6,2},{7,3},{8,12},{9,13},{10,... | collective-permute-start | bytes 98312 | tf_op jit(solution)/shard_map/ppermute | solution.py:17
  52.4 0.6 reduce_sum.19
  53.0 1.7 %collective-permute-done.10 = f32[2,4096]{1,0:T(2,128)S(1)} collective-permute-done((f32[2,4096]{1,0:T(2,128)S(1)}, f32[2,4096]{1,0:T(2,128)S(1)}, u32[]{:S(2)}, u32[]{:S(2)}) %collective-permute-start.10) | collective-permute-done | bytes 32800 | tf_op jit(solution)/shard_map/ppermute | solution.py:17
  54.8 2.1 %collective-permute-start.11 = (bf16[1,4096]{1,0:T(2,128)(2,1)S(1)}, bf16[1,4096]{1,0:T(2,128)(2,1)S(1)}, u32[]{:S(2)}, u32[]{:S(2)}) collective-permute-start(bf16[1,4096]{1,0:T(2,128)(2,1)S(1)} %get-tuple-element.19), channel_id=1, source_target_pairs={{0,8},{1,9},{2,10},{3,11},{4,12},{5,13},{6,14},{7,15},{8,0},{9,1},... | collective-permute-start | bytes 24584 | tf_op jit(solution)/shard_map/ppermute | solution.py:17
  56.9 0.1 collective-permute-start.7
  57.0 0.5 collective-permute-start.6
  57.5 2.0 %collective-permute-done.11 = bf16[1,4096]{1,0:T(2,128)(2,1)S(1)} collective-permute-done((bf16[1,4096]{1,0:T(2,128)(2,1)S(1)}, bf16[1,4096]{1,0:T(2,128)(2,1)S(1)}, u32[]{:S(2)}, u32[]{:S(2)}) %collective-permute-start.11) | collective-permute-done | bytes 8224 | tf_op jit(solution)/shard_map/ppermute | solution.py:17
  59.5 0.1 pad_maximum_fusion.3
  59.6 0.7 convert_element_type.29
  60.2 0.1 collective-permute-done.7
  60.3 4.7 %collective-permute-done.6 = bf16[768,128]{0,1:T(8,128)(2,1)S(1)} collective-permute-done((bf16[768,128]{0,1:T(8,128)(2,1)S(1)}, bf16[768,128]{0,1:T(8,128)(2,1)S(1)}, u32[]{:S(2)}, u32[]{:S(2)}) %collective-permute-start.6) | collective-permute-done | bytes 196640 | tf_op jit(solution)/shard_map/ppermute | solution.py:27
  65.0 0.1 pad_maximum_fusion.1
  65.1 0.6 copy.31
  65.7 8.1 %gather_fusion.1 = bf16[192,128,128]{2,1,0:T(8,128)(2,1)} fusion(bf16[28,128,128]{2,1,0:T(8,128)(2,1)S(1)} %bitcast.50, s32[1024]{0:T(1024)S(1)} %pad_clamp_fusion), kind=kCustom, calls=%fused_computation.1 | custom fusion | bytes 12583680 | tf_op jit(solution)/shard_map/gather | solution.py:79
  73.8 6.4 %fusion.16 = f32[16,128,128,1]{1,2,3,0:T(8,128)S(1)} fusion(bf16[16,12,128,128]{3,2,1,0:T(8,128)(2,1)} %param.13, bf16[16,12,128,128]{3,2,1,0:T(8,128)(2,1)} %bitcast.52), kind=kOutput, calls=%fused_computation.52 | convolution fusion | flops 805306368 | bytes 13631488 | tf_op jit(solution)/shard_map/rkij,rkjb->rib/dot_general | solution.py:80
  80.2 1.3 %copy.40 = f32[2048,128]{0,1:T(8,128)} copy(f32[2048,128]{1,0:T(8,128)S(1)} %bitcast.55) | data formatting | bytes 2097152 | tf_op jit(solution)/shard_map/reshape | solution.py:82
  81.6 4.3 %multiply_reduce_fusion = (f32[128]{0:T(128)S(1)}, f32[2048,128]{0,1:T(8,128)S(1)}, f32[2048,128]{0,1:T(8,128)}) fusion(f32[2048,128]{0,1:T(8,128)} %get-tuple-element.23, f32[2048]{0:T(1024)S(1)} %copy-done.4, f32[2048,128]{0,1:T(8,128)} %copy.29, f32[2048,128]{0,1:T(8,128)S(1)} %copy.34, f32[2048]{0:T(1024)S(1)} %copy-done.6, f32[2048]{0:T(1024)S(1)} %copy-done.8, ...), kind=kOutput, calls=%fused_computation.11 | convolution fusion | flops 75497344 | bytes 6889984 | tf_op jit(solution)/shard_map/dot_general | solution.py:87
  85.9 2.5 %copy.36 = f32[2048,128]{1,0:T(8,128)} copy(f32[2048,128]{0,1:T(8,128)} %get-tuple-element.13) | data formatting | bytes 2097152
  88.5 1.3 %copy.37 = f32[2048,128]{1,0:T(8,128)} copy(f32[2048,128]{0,1:T(8,128)S(1)} %get-tuple-element.12) | data formatting | bytes 2097152
  89.8 30.1 %all-reduce = (f32[128]{0:T(128)S(1)}, f32[]{:T(128)}) all-reduce(f32[128]{0:T(128)S(1)} %get-tuple-element.11, f32[]{:T(128)} %reduce_sum.19), channel_id=1, replica_groups=mesh['member'=2,'patch'=16] {'patch'}, use_global_device_ids=true, to_apply=%region_1.2 | all-reduce | flops 129 | bytes 1032 | tf_op jit(solution)/shard_map/psum | solution.py:111
  119.9 1.1 add_sqrt_fusion
  (50 shorter events, 0.5 us)
Async XLA Ops:
  0.6 40.7 %copy-start = (bf16[4,32,2048]{2,1,0:T(8,128)(2,1)S(1)}, bf16[4,32,2048]{2,1,0:T(8,128)(2,1)}, u32[]{:S(2)}) copy-start(bf16[4,32,2048]{2,1,0:T(8,128)(2,1)} %param.16) | copy-start | bytes 1572868
  3.8 6.3 %collective-permute-start.2 = (f32[4,4096]{1,0:T(4,128)S(1)}, f32[4,4096]{1,0:T(4,128)S(1)}, u32[]{:S(2)}, u32[]{:S(2)}) collective-permute-start(f32[4,4096]{1,0:T(4,128)S(1)} %reshape.65), channel_id=1, source_target_pairs={{0,1},{1,0},{2,3},{3,2},{4,5},{5,4},{6,7},{7,6},{8,9},{9,8},{10,11... | collective-permute-start | bytes 196616 | tf_op jit(solution)/shard_map/ppermute | solution.py:17
  4.4 20.4 %collective-permute-start.1 = (bf16[768,128]{0,1:T(8,128)(2,1)S(1)}, bf16[768,128]{0,1:T(8,128)(2,1)S(1)}, u32[]{:S(2)}, u32[]{:S(2)}) collective-permute-start(bf16[768,128]{0,1:T(8,128)(2,1)S(1)} %get-tuple-element.17), channel_id=1, source_target_pairs={{1,0},{2,1},{3,2},{4,3},{5,4},{6,5},{7,6},{8,7},{9,8},{10,9},{11,1... | collective-permute-start | bytes 589832 | tf_op jit(solution)/shard_map/ppermute | solution.py:29
  10.1 14.7 %collective-permute-start = (bf16[768,128]{0,1:T(8,128)(2,1)S(1)}, bf16[768,128]{0,1:T(8,128)(2,1)S(1)}, u32[]{:S(2)}, u32[]{:S(2)}) collective-permute-start(bf16[768,128]{0,1:T(8,128)(2,1)S(1)} %get-tuple-element.16), channel_id=1, source_target_pairs={{0,1},{1,2},{2,3},{3,4},{4,5},{5,6},{6,7},{7,8},{8,9},{9,10},{10,1... | collective-permute-start | bytes 589832 | tf_op jit(solution)/shard_map/ppermute | solution.py:27
  10.2 4.3 %collective-permute-start.3 = (f32[3,4096]{1,0:T(4,128)S(1)}, f32[3,4096]{1,0:T(4,128)S(1)}, u32[]{:S(2)}, u32[]{:S(2)}) collective-permute-start(f32[3,4096]{1,0:T(4,128)S(1)} %slice_add_fusion.1), channel_id=1, source_target_pairs={{0,2},{1,3},{2,0},{3,1},{4,6},{5,7},{6,4},{7,5},{8,10},{9,11},{10,... | collective-permute-start | bytes 147464 | tf_op jit(solution)/shard_map/ppermute | solution.py:17
  14.5 4.0 %collective-permute-start.4 = (f32[2,4096]{1,0:T(2,128)S(1)}, f32[2,4096]{1,0:T(2,128)S(1)}, u32[]{:S(2)}, u32[]{:S(2)}) collective-permute-start(f32[2,4096]{1,0:T(2,128)S(1)} %slice_add_fusion.3), channel_id=1, source_target_pairs={{0,4},{1,5},{2,6},{3,7},{4,0},{5,1},{6,2},{7,3},{8,12},{9,13},{10,... | collective-permute-start | bytes 98312 | tf_op jit(solution)/shard_map/ppermute | solution.py:17
  18.5 5.4 %collective-permute-start.5 = (bf16[1,4096]{1,0:T(2,128)(2,1)S(1)}, bf16[1,4096]{1,0:T(2,128)(2,1)S(1)}, u32[]{:S(2)}, u32[]{:S(2)}) collective-permute-start(bf16[1,4096]{1,0:T(2,128)(2,1)S(1)} %get-tuple-element.21), channel_id=1, source_target_pairs={{0,8},{1,9},{2,10},{3,11},{4,12},{5,13},{6,14},{7,15},{8,0},{9,1},... | collective-permute-start | bytes 24584 | tf_op jit(solution)/shard_map/ppermute | solution.py:17
  33.5 7.8 %copy-start.3 = (bf16[128,128]{1,0:T(8,128)(2,1)S(1)}, bf16[128,128]{1,0:T(8,128)(2,1)}, u32[]{:S(2)}) copy-start(bf16[128,128]{1,0:T(8,128)(2,1)} %convert_element_type.27) | copy-start | bytes 98308
  33.5 7.8 %copy-start.5 = (f32[2048]{0:T(1024)S(1)}, f32[2048]{0:T(1024)}, u32[]{:S(2)}) copy-start(f32[2048]{0:T(1024)} %param.19) | copy-start | bytes 24580
  33.5 7.8 %copy-start.7 = (f32[2048]{0:T(1024)S(1)}, f32[2048]{0:T(1024)}, u32[]{:S(2)}) copy-start(f32[2048]{0:T(1024)} %param.20) | copy-start | bytes 24580
  33.5 7.8 %copy-start.9 = (f32[2048]{0:T(1024)S(1)}, f32[2048]{0:T(1024)}, u32[]{:S(2)}) copy-start(f32[2048]{0:T(1024)} %param.18) | copy-start | bytes 24580
  33.5 7.8 %copy-start.11 = (f32[2048]{0:T(1024)S(1)}, f32[2048]{0:T(1024)}, u32[]{:S(2)}) copy-start(f32[2048]{0:T(1024)} %param.17) | copy-start | bytes 24580
  40.0 4.7 %copy-start.1 = (bf16[4,32,2048]{2,1,0:T(8,128)(2,1)S(1)}, bf16[4,32,2048]{2,1,0:T(8,128)(2,1)}, u32[]{:S(2)}) copy-start(bf16[4,32,2048]{2,1,0:T(8,128)(2,1)} %param.15) | copy-start | bytes 1572868
  40.0 12.4 %copy-start.4 = (f32[2048]{0:T(1024)S(1)}, f32[2048]{0:T(1024)}, u32[]{:S(2)}) copy-start(f32[2048]{0:T(1024)} %param.21) | copy-start | bytes 24580
  45.0 1.3 %collective-permute-start.8 = (f32[4,4096]{1,0:T(4,128)S(1)}, f32[4,4096]{1,0:T(4,128)S(1)}, u32[]{:S(2)}, u32[]{:S(2)}) collective-permute-start(f32[4,4096]{1,0:T(4,128)S(1)} %reshape.69), channel_id=1, source_target_pairs={{0,1},{1,0},{2,3},{3,2},{4,5},{5,4},{6,7},{7,6},{8,9},{9,8},{10,11... | collective-permute-start | bytes 196616 | tf_op jit(solution)/shard_map/ppermute | solution.py:17
  46.4 4.3 %collective-permute-start.9 = (f32[3,4096]{1,0:T(4,128)S(1)}, f32[3,4096]{1,0:T(4,128)S(1)}, u32[]{:S(2)}, u32[]{:S(2)}) collective-permute-start(f32[3,4096]{1,0:T(4,128)S(1)} %slice_add_fusion), channel_id=1, source_target_pairs={{0,2},{1,3},{2,0},{3,1},{4,6},{5,7},{6,4},{7,5},{8,10},{9,11},{10,... | collective-permute-start | bytes 147464 | tf_op jit(solution)/shard_map/ppermute | solution.py:17
  50.8 4.0 %collective-permute-start.10 = (f32[2,4096]{1,0:T(2,128)S(1)}, f32[2,4096]{1,0:T(2,128)S(1)}, u32[]{:S(2)}, u32[]{:S(2)}) collective-permute-start(f32[2,4096]{1,0:T(2,128)S(1)} %slice_add_fusion.2), channel_id=1, source_target_pairs={{0,4},{1,5},{2,6},{3,7},{4,0},{5,1},{6,2},{7,3},{8,12},{9,13},{10,... | collective-permute-start | bytes 98312 | tf_op jit(solution)/shard_map/ppermute | solution.py:17
  54.8 4.7 %collective-permute-start.11 = (bf16[1,4096]{1,0:T(2,128)(2,1)S(1)}, bf16[1,4096]{1,0:T(2,128)(2,1)S(1)}, u32[]{:S(2)}, u32[]{:S(2)}) collective-permute-start(bf16[1,4096]{1,0:T(2,128)(2,1)S(1)} %get-tuple-element.19), channel_id=1, source_target_pairs={{0,8},{1,9},{2,10},{3,11},{4,12},{5,13},{6,14},{7,15},{8,0},{9,1},... | collective-permute-start | bytes 24584 | tf_op jit(solution)/shard_map/ppermute | solution.py:17
  56.9 3.4 %collective-permute-start.7 = (bf16[768,128]{0,1:T(8,128)(2,1)S(1)}, bf16[768,128]{0,1:T(8,128)(2,1)S(1)}, u32[]{:S(2)}, u32[]{:S(2)}) collective-permute-start(bf16[768,128]{0,1:T(8,128)(2,1)S(1)} %get-tuple-element.15), channel_id=1, source_target_pairs={{1,0},{2,1},{3,2},{4,3},{5,4},{6,5},{7,6},{8,7},{9,8},{10,9},{11,1... | collective-permute-start | bytes 589832 | tf_op jit(solution)/shard_map/ppermute | solution.py:29
  57.0 8.0 %collective-permute-start.6 = (bf16[768,128]{0,1:T(8,128)(2,1)S(1)}, bf16[768,128]{0,1:T(8,128)(2,1)S(1)}, u32[]{:S(2)}, u32[]{:S(2)}) collective-permute-start(bf16[768,128]{0,1:T(8,128)(2,1)S(1)} %get-tuple-element.14), channel_id=1, source_target_pairs={{0,1},{1,2},{2,3},{3,4},{4,5},{5,6},{6,7},{7,8},{8,9},{9,10},{10,1... | collective-permute-start | bytes 589832 | tf_op jit(solution)/shard_map/ppermute | solution.py:27
  73.8 7.8 %copy-start.2 = (bf16[128,128]{1,0:T(8,128)(2,1)S(1)}, bf16[128,128]{1,0:T(8,128)(2,1)}, u32[]{:S(2)}) copy-start(bf16[128,128]{1,0:T(8,128)(2,1)} %convert_element_type.29) | copy-start | bytes 98308
  73.8 7.8 %copy-start.6 = (f32[2048]{0:T(1024)S(1)}, f32[2048]{0:T(1024)}, u32[]{:S(2)}) copy-start(f32[2048]{0:T(1024)} %param.19) | copy-start | bytes 24580
  73.8 7.8 %copy-start.8 = (f32[2048]{0:T(1024)S(1)}, f32[2048]{0:T(1024)}, u32[]{:S(2)}) copy-start(f32[2048]{0:T(1024)} %param.20) | copy-start | bytes 24580
  73.8 7.8 %copy-start.10 = (f32[2048]{0:T(1024)S(1)}, f32[2048]{0:T(1024)}, u32[]{:S(2)}) copy-start(f32[2048]{0:T(1024)} %param.18) | copy-start | bytes 24580
  73.8 7.8 %copy-start.12 = (f32[2048]{0:T(1024)S(1)}, f32[2048]{0:T(1024)}, u32[]{:S(2)}) copy-start(f32[2048]{0:T(1024)} %param.17) | copy-start | bytes 24580
where the time goes:
time: 121 us
  blocking collectives  30.1 us (25%)
  local copies, waits for them, and re-layouts  29.6 us (24%)
  matrix products  22.2 us (18%)
  waiting for transfers between devices  18.8 us (16%)
  starting transfers between devices  16.1 us (13%)
  other arithmetic  3.17 us (3%)
    psum x1, blocking collectives, on_device(): totals, area_total = lax.psum((area_terms, jnp.sum(triangle_area)), 'patch')  30.1 us
    gather x2, local copies, waits for them, and re-layouts, section_rates(): chosen = column_blocks[position]  16.1 us
    ppermute x8, waiting for transfers between devices, partner_2(): return lax.ppermute(value, axis, pairs)  14 us
    dot_general x2, matrix products, section_rates(): jnp.einsum('rkij,rkjb->rib', near_blocks, chosen, preferred_element_type=...  12.9 us
    ppermute x8, starting transfers between devices, partner_2(): return lax.ppermute(value, axis, pairs)  9.84 us
    unnamed x30, local copies, waits for them, and re-layouts  8.04 us
    dot_general x2, matrix products, section_rates(): lax.dot_general(coupling, coupled, (((0,), (0,)), ((), ())), preferred_el...  7.7 us
    ppermute x2, starting transfers between devices, padded(): lax.ppermute(head, axis, [((i + 1) % count, i) for i in range(count)])  5.77 us
  transfers between devices with their start and end apart: 12, of which 8 were waited for; matrix products, arithmetic and copies ran while one was open for 5% of the time, Pallas kernels for 0%

commit v1 on v0

v1 whole, which is shorter than its diff:
```python
import functools

import jax
import jax.numpy as jnp
from jax import lax
from jax.experimental import pallas as pl
from jax.experimental.pallas import tpu as pltpu
from jax.sharding import PartitionSpec as P

REACH = 6
WIDE = 2 * REACH + 1
GROUP = 4
PIECES = 4
HALF = REACH // 2

step_size = 0.1
damping = 0.5
error_scale = 0.01
MESH = pl.DeviceIdType.MESH


def flipped(me, mask):
    other = me
    bit = 1
    while bit <= mask:
        if mask & bit:
            other = other + bit * (1 - 2 * ((me // bit) % 2))
        bit *= 2
    return other


def kernel(
    n,
    rows,
    size,
    levels,
    rank,
    index_ref,
    log_rate,
    log_state,
    near,
    basis,
    coupling,
    stiff_in,
    plate_in,
    direct_in,
    evolve_in,
    area_in,
    rate_out,
    state_out,
    error_out,
    *scratch,
):
    near_bufs = scratch[:PIECES]
    (
        p_buf,
        s_buf,
        basis_buf,
        coupling_buf,
        coupling_t,
        vectors,
        columns,
        v_buf,
        kp_buf,
        ks_buf,
        acc,
        ext,
        send_a,
        recv_a,
        send_b,
        recv_b,
        err_send,
        err_recv,
        p_res,
        s_res,
        in_sems,
        near_sems,
        out_sems,
        halo_send,
        halo_recv,
        a_send,
        a_recv,
        b_send,
        b_recv,
        e_send,
        e_recv,
    ) = scratch[PIECES:]
    me = lax.axis_index("patch")
    right = lax.rem(me + 1, n)
    left = lax.rem(me + n - 1, n)
    per_piece = rows // PIECES
    near_count = near.shape[0] // rows
    groups = n // GROUP

    barrier = pltpu.get_barrier_semaphore()
    for mask in range(1, n):
        pl.semaphore_signal(
            barrier, inc=1, device_id={"patch": flipped(me, mask)}, device_id_type=MESH
        )

    def span(first, count=1):
        return pl.ds(first * size, count * size)

    loads = [
        pltpu.make_async_copy(log_rate, p_buf, in_sems.at[0]),
        pltpu.make_async_copy(basis, basis_buf, in_sems.at[1]),
        pltpu.make_async_copy(coupling, coupling_buf, in_sems.at[2]),
        pltpu.make_async_copy(log_state, s_buf, in_sems.at[3]),
    ]
    vector_loads = [
        pltpu.make_async_copy(source, vectors.at[pl.ds(i * rows, rows)], in_sems.at[4 + i])
        for i, source in enumerate((stiff_in, plate_in, direct_in, evolve_in, area_in))
    ]
    near_loads = [
        pltpu.make_async_copy(
            near.at[pl.ds(q * per_piece * near_count, per_piece * near_count)],
            near_bufs[q].at[pl.ds(0, per_piece * near_count)],
            near_sems.at[q],
        )
        for q in range(PIECES)
    ]
    loads[0].start()
    loads[1].start()
    for load in vector_loads:
        load.start()
    loads[2].start()
    for load in near_loads:
        load.start()
    loads[3].start()
    used = 5 * rows
    if vectors.shape[0] > used:
        vectors[used:, :] = jnp.zeros((vectors.shape[0] - used, size), jnp.float32)
    for q in range(PIECES):
        near_bufs[q][per_piece * near_count] = jnp.zeros((size, size), jnp.bfloat16)

    def halo_copy(section, way, piece):
        if way == 0:
            first, target, peer = HALF * piece, rows + REACH + HALF * piece, left
        else:
            first = rows - HALF * (piece + 1)
            target, peer = REACH - HALF * (piece + 1), right
        return pltpu.make_async_remote_copy(
            src_ref=ext.at[section, span(REACH + first, HALF)],
            dst_ref=ext.at[section, span(target, HALF)],
            send_sem=halo_send.at[section, way, piece],
            recv_sem=halo_recv.at[section, way, piece],
            device_id={"patch": peer},
            device_id_type=MESH,
        )

    def a_copy(section, mask):
        first = 0 if mask == 1 else rank
        part = pl.ds(first, levels * rank - first)
        return pltpu.make_async_remote_copy(
            src_ref=send_a.at[section, part],
            dst_ref=recv_a.at[section, mask - 1, part],
            send_sem=a_send.at[section, mask - 1],
            recv_sem=a_recv.at[section, mask - 1],
            device_id={"patch": flipped(me, mask)},
            device_id_type=MESH,
        )

    def b_copy(section, mask):
        level = mask.bit_length() + 1
        return pltpu.make_async_remote_copy(
            src_ref=send_b.at[section, pl.ds((level - 2) * rank, rank)],
            dst_ref=recv_b.at[section, mask - 1],
            send_sem=b_send.at[section, mask - 1],
            recv_sem=b_recv.at[section, mask - 1],
            device_id={"patch": flipped(me, mask * GROUP)},
            device_id_type=MESH,
        )

    def error_copy(mask):
        return pltpu.make_async_remote_copy(
            src_ref=err_send,
            dst_ref=err_recv.at[mask - 1],
            send_sem=e_send.at[mask - 1],
            recv_sem=e_recv.at[mask - 1],
            device_id={"patch": flipped(me, mask)},
            device_id_type=MESH,
        )

    def near_lhs(r, first, last):
        buf = near_bufs[r // per_piece]
        return [buf[index_ref[r * WIDE + o]] for o in range(first, last)]

    def column(vector, r):
        j = vector * rows + r
        return columns[:, j : j + 1]

    def project(section):
        projected = jnp.dot(
            basis_buf[...], ext[section, span(REACH, rows)], preferred_element_type=jnp.float32
        )
        send_a[section] = projected.astype(jnp.bfloat16)
        for mask in range(1, GROUP):
            a_copy(section, mask).start()
        return projected

    def local_near(section, some_rows):
        for r in some_rows:
            if section == 0 and r % per_piece == 0:
                near_loads[r // per_piece].wait()
            first = max(0, REACH - r)
            last = min(WIDE, rows + REACH - r)
            acc[span(r)] = jnp.dot(
                jnp.concatenate(near_lhs(r, first, last), axis=1),
                ext[section, span(r + first, last - first)],
                preferred_element_type=jnp.float32,
            )

    def exchange_groups(section, projected):
        for mask in range(1, GROUP):
            a_copy(section, mask).wait_recv()
        if groups > 1:
            total = projected[2 * rank :]
            for mask in range(1, GROUP):
                total = total + recv_a[section, mask - 1, pl.ds(2 * rank, (levels - 2) * rank)].astype(
                    jnp.float32
                )
            send_b[section] = total.astype(jnp.bfloat16)
            for mask in range(1, groups):
                b_copy(section, mask).start()

    def sibling_sums(section):
        parts = [recv_a[section, 0, pl.ds(0, rank)]]
        parts.append(
            (
                recv_a[section, 1, pl.ds(rank, rank)].astype(jnp.float32)
                + recv_a[section, 2, pl.ds(rank, rank)].astype(jnp.float32)
            ).astype(jnp.bfloat16)
        )
        for mask in range(1, groups):
            b_copy(section, mask).wait_recv()
        for level in range(2, levels):
            low = 2 ** (level - 2)
            total = recv_b[section, low - 1].astype(jnp.float32)
            for mask in range(low + 1, 2 * low):
                total = total + recv_b[section, mask - 1].astype(jnp.float32)
            parts.append(total.astype(jnp.bfloat16))
        return jnp.concatenate(parts, axis=0)

    def rates(section, r, coupled, state):
        lhs, rhs = [], []
        low, high = max(0, REACH - r), min(WIDE, rows + REACH - r)
        if low > 0:
            lhs += near_lhs(r, 0, low)
            rhs.append(ext[section, span(r, low)])
        if high < WIDE:
            lhs += near_lhs(r, high, WIDE)
            rhs.append(ext[section, span(r + high, WIDE - high)])
        lhs.append(coupling_t[span(r)])
        rhs.append(coupled)
        if len(rhs) > 1:
            lhs, rhs = jnp.concatenate(lhs, axis=1), jnp.concatenate(rhs, axis=0)
        else:
            lhs, rhs = lhs[0], rhs[0]
        stress = acc[span(r)] + jnp.dot(lhs, rhs, preferred_element_type=jnp.float32)
        velocity = v_buf[span(r)]
        state_rate = jnp.exp(-state) - velocity
        stress_rate = column(0, r) * (column(1, r) - velocity) - stress
        rate = (stress_rate - column(3, r) * state_rate) / (column(2, r) + damping * velocity)
        return rate, state_rate

    edge_order = (
        list(range(HALF))
        + list(range(rows - HALF, rows))
        + list(range(HALF, REACH))
        + list(range(rows - REACH, rows - HALF))
    )
    order = edge_order + list(range(REACH, rows - REACH))
    sends_after = {
        HALF - 1: [(0, 0)],
        rows - 1: [(1, 0)],
        REACH - 1: [(0, 1)],
        rows - HALF - 1: [(1, 1)],
    }

    loads[0].wait()

    def first_velocity(first, count):
        velocity = jnp.exp(p_buf[span(first, count)])
        v_buf[span(first, count)] = velocity
        ext[0, span(REACH + first, count)] = velocity.astype(jnp.bfloat16)

    first_velocity(0, REACH)
    first_velocity(rows - REACH, REACH)
    pl.semaphore_wait(barrier, n - 1)
    for piece in range(2):
        for way in range(2):
            halo_copy(0, way, piece).start()
    first_velocity(REACH, rows - 2 * REACH)
    loads[1].wait()
    projected = project(0)

    for load in vector_loads:
        load.wait()
    columns[...] = vectors[...].T
    loads[2].wait()
    for r in range(rows):
        coupling_t[span(r)] = coupling_buf[:, r * size : (r + 1) * size].T
    half_rows = rows // 2
    local_near(0, range(half_rows))
    exchange_groups(0, projected)
    local_near(0, range(half_rows, rows))
    loads[3].wait()
    for piece in range(2):
        for way in range(2):
            halo_copy(0, way, piece).wait_recv()
    coupled = sibling_sums(0)
    for r in order:
        state = s_buf[span(r)]
        rate, state_rate = rates(0, r, coupled, state)
        kp_buf[span(r)] = rate
        ks_buf[span(r)] = state_rate
        velocity = jnp.exp(p_buf[span(r)] + step_size * rate)
        v_buf[span(r)] = velocity
        ext[1, span(REACH + r)] = velocity.astype(jnp.bfloat16)
        for way, piece in sends_after.get(r, ()):
            halo_copy(1, way, piece).start()

    projected = project(1)
    local_near(1, range(half_rows))
    exchange_groups(1, projected)
    local_near(1, range(half_rows, rows))
    for piece in range(2):
        for way in range(2):
            halo_copy(1, way, piece).wait_recv()
    coupled = sibling_sums(1)
    half_step = 0.5 * step_size
    scale = half_step / error_scale
    weighted = jnp.zeros((8, v_buf.shape[1]), jnp.float32)
    results = []
    for r in order:
        state_one = ks_buf[span(r)]
        rate_one = kp_buf[span(r)]
        state = s_buf[span(r)]
        rate, state_rate = rates(1, r, coupled, state + step_size * state_one)
        p_res[span(r)] = p_buf[span(r)] + half_step * (rate_one + rate)
        s_res[span(r)] = state + half_step * (state_one + state_rate)
        for i, (source, target) in enumerate(((p_res, rate_out), (s_res, state_out))):
            store = pltpu.make_async_copy(
                source.at[span(r)], target.at[span(r)], out_sems.at[i, r]
            )
            store.start()
            results.append(store)
        rate_error = scale * (rate - rate_one)
        state_error = scale * (state_rate - state_one)
        squares = column(4, r) * (rate_error * rate_error + state_error * state_error)
        weighted = weighted + jnp.sum(squares.reshape(-1, 8, squares.shape[1]), axis=0)

    area = jnp.sum(vectors[4 * rows : 5 * rows, :])
    err_send[0:1, :] = jnp.sum(weighted, axis=0, keepdims=True)
    err_send[1:2, :] = jnp.full((1, weighted.shape[1]), area, jnp.float32)
    err_send[2:8, :] = jnp.zeros((6, weighted.shape[1]), jnp.float32)
    for mask in range(1, n):
        error_copy(mask).start()
    for section in range(2):
        for piece in range(2):
            for way in range(2):
                halo_copy(section, way, piece).wait_send()
        for mask in range(1, GROUP):
            a_copy(section, mask).wait_send()
        for mask in range(1, groups):
            b_copy(section, mask).wait_send()
    for mask in range(1, n):
        error_copy(mask).wait_recv()
    both = err_send[...]
    for mask in range(1, n):
        both = both + err_recv[mask - 1]
    error_out[...] = jnp.sqrt(both[0:1] / both[1:2] + 1e-06)
    for mask in range(1, n):
        error_copy(mask).wait_send()
    for store in results:
        store.wait()


def on_device(
    log_rate,
    log_state,
    near_blocks,
    near_columns,
    far_basis,
    far_coupling,
    self_stiffness,
    plate_rate,
    direct_effect,
    evolution_effect,
    triangle_area,
):
    row_count, scenarios = log_rate.shape
    rows, near_count, size, _ = near_blocks.shape
    n = lax.axis_size("patch")
    levels, rank, _ = far_basis.shape
    total_blocks = n * rows
    first_block = lax.axis_index("patch") * rows
    local_index = jnp.arange(rows, dtype=jnp.int32)
    per_piece = rows // PIECES
    slot = (near_columns - (first_block + local_index)[:, None] + total_blocks + REACH) % total_blocks
    hit = slot[:, None, :] == jnp.arange(WIDE, dtype=jnp.int32)[None, :, None]
    none = per_piece * near_count
    place = (local_index % per_piece)[:, None, None] * near_count + jnp.arange(
        near_count, dtype=jnp.int32
    )
    index = none + jnp.sum(jnp.where(hit, place - none, 0), axis=2)

    def by_block(vector):
        return vector.reshape(rows, size)

    padded_vectors = -(-5 * rows // 128) * 128
    far_rows = levels * rank
    groups = n // GROUP
    ext_rows = (rows + 2 * REACH) * size
    f32, bf16 = jnp.float32, jnp.bfloat16
    dma = pltpu.SemaphoreType.DMA
    anywhere = pl.BlockSpec(memory_space=pl.ANY)
    new_rate, new_state, error = pl.pallas_call(
        functools.partial(kernel, n, rows, size, levels, rank),
        out_shape=(
            jax.ShapeDtypeStruct((row_count, scenarios), f32),
            jax.ShapeDtypeStruct((row_count, scenarios), f32),
            jax.ShapeDtypeStruct((1, scenarios), f32),
        ),
        in_specs=[pl.BlockSpec(memory_space=pltpu.SMEM)] + [anywhere] * 10,
        out_specs=(anywhere, anywhere, pl.BlockSpec(memory_space=pltpu.VMEM)),
        scratch_shapes=[
            pltpu.VMEM((per_piece * near_count + 1, size, size), bf16) for _ in range(PIECES)
        ]
        + [
            pltpu.VMEM((row_count, scenarios), f32),
            pltpu.VMEM((row_count, scenarios), f32),
            pltpu.VMEM((far_rows, row_count), bf16),
            pltpu.VMEM((far_rows, row_count), bf16),
            pltpu.VMEM((row_count, far_rows), bf16),
            pltpu.VMEM((padded_vectors, size), f32),
            pltpu.VMEM((size, padded_vectors), f32),
            pltpu.VMEM((row_count, scenarios), f32),
            pltpu.VMEM((row_count, scenarios), f32),
            pltpu.VMEM((row_count, scenarios), f32),
            pltpu.VMEM((row_count, scenarios), f32),
            pltpu.VMEM((2, ext_rows, scenarios), bf16),
            pltpu.VMEM((2, far_rows, scenarios), bf16),
            pltpu.VMEM((2, GROUP - 1, far_rows, scenarios), bf16),
            pltpu.VMEM((2, (levels - 2) * rank, scenarios), bf16),
            pltpu.VMEM((2, groups - 1, rank, scenarios), bf16),
            pltpu.VMEM((8, scenarios), f32),
            pltpu.VMEM((n - 1, 8, scenarios), f32),
            pltpu.VMEM((row_count, scenarios), f32),
            pltpu.VMEM((row_count, scenarios), f32),
            dma((9,)),
            dma((PIECES,)),
            dma((2, rows)),
            dma((2, 2, 2)),
            dma((2, 2, 2)),
            dma((2, GROUP - 1)),
            dma((2, GROUP - 1)),
            dma((2, groups - 1)),
            dma((2, groups - 1)),
            dma((n - 1,)),
            dma((n - 1,)),
        ],
        compiler_params=pltpu.CompilerParams(
            collective_id=0, has_side_effects=True, vmem_limit_bytes=48 * 1024 * 1024
        ),
    )(
        index.reshape(-1),
        log_rate,
        log_state,
        near_blocks.reshape(rows * near_count, size, size),
        far_basis.reshape(far_rows, row_count),
        far_coupling.reshape(far_rows, row_count),
        by_block(self_stiffness),
        by_block(plate_rate),
        by_block(direct_effect),
        by_block(evolution_effect),
        by_block(triangle_area),
    )
    return (new_rate, new_state, error.reshape(-1))


def solution(mesh):
    in_specs = (
        P(("member", "patch"), None),
        P(("member", "patch"), None),
        P(("member", "patch"), None, None, None),
        P(("member", "patch"), None),
        P("member", None, "patch"),
        P("member", None, "patch"),
        P(("member", "patch")),
        P(("member", "patch")),
        P(("member", "patch")),
        P(("member", "patch")),
        P(("member", "patch")),
    )
    out_specs = (P(("member", "patch"), None), P(("member", "patch"), None), P("member"))
    return jax.shard_map(
        on_device, mesh=mesh, in_specs=in_specs, out_specs=out_specs, check_vma=False
    )
```

time: 121 us -> 52 us (0.43)
  Pallas kernels: 0 us -> 39.2 us
  blocking collectives: 30.1 us -> 0 us
  matrix products: 22.2 us -> 0 us
  local copies, waits for them, and re-layouts: 29.6 us -> 10.6 us
  waiting for transfers between devices: 18.8 us -> 0 us
  starting transfers between devices: 16.1 us -> 0 us
  other arithmetic: 3.17 us -> 0.91 us
    pallas_call x0 -> x1, Pallas kernels: none -> 39.2 us  [on_device(): pl.pallas_call(functools.partial(kernel, n, rows, size, levels, rank), ou...]
    psum x1 -> x0, blocking collectives: 30.1 us -> none  [on_device(): totals, area_total = lax.psum((area_terms, jnp.sum(triangle_area)), 'patch')]
    dot_general x6 -> x0, matrix products: 22.2 us -> none  [the longest x2 12.9 us: section_rates(): jnp.einsum('rkij,rkjb->rib', near_blocks, chosen, preferred_element_type=...]
    ppermute x12 -> x0, waiting for transfers between devices: 18.8 us -> none  [the longest x8 14 us: partner_2(): return lax.ppermute(value, axis, pairs)]
    gather x2 -> x0, local copies, waits for them, and re-layouts: 16.1 us -> none  [section_rates(): chosen = column_blocks[position]]
    ppermute x12 -> x0, starting transfers between devices: 16.1 us -> none  [the longest x8 9.84 us: partner_2(): return lax.ppermute(value, axis, pairs)]
    reshape x4 -> x0, local copies, waits for them, and re-layouts: 2.69 us -> none  [the longest x2 2.64 us: section_rates(): near_term = jnp.einsum('rkij,rkjb->rib', near_blocks, chosen, preferred_e...]
    unnamed x30 -> x21, local copies, waits for them, and re-layouts: 8.04 us -> 10.5 us
  transfers between devices with their start and end apart: 12 -> 0, of which waited for: 8 -> 0; matrix products, arithmetic and copies ran while one was open for 5% -> 0% of each run, Pallas kernels for 0% -> 0%
where the time goes in v1:
time: 52 us; the launch traced here: 51.5 us
  Pallas kernels  39.2 us (75%)
  local copies, waits for them, and re-layouts  10.6 us (20%)
  other arithmetic  0.91 us (2%)
  between operations  0.7 us (1%)
    pallas_call x1, Pallas kernels, on_device(): pl.pallas_call(functools.partial(kernel, n, rows, size, levels, rank), ou...  39.2 us
    unnamed x21, local copies, waits for them, and re-layouts  10.5 us

profile of v1, /device:TPU:0, one launch (start us, length us, event | category | flops | bytes accessed | tf_op | source)
XLA Modules:
  0.0 51.5 jit_solution(5392245154304336177)
XLA Ops:
  0.7 0.8 %add_select_fusion = s32[16,12]{1,0:T(8,128)S(1)} fusion(s32[16,12]{1,0:T(8,128)} %param.14, s32[16]{0:T(128)S(1)} %iota_add_fusion), kind=kLoop, calls=%fused_computation.2 | loop fusion | flops 2496 | bytes 1600 | tf_op jit(solution)/shard_map/jit(remainder)/select_n | solution.py:400
  1.4 0.1 copy.14
  1.5 0.1 select_reduce_fusion
  1.7 0.1 add.81.index_ref
  1.8 0.0 copy-start
  1.8 1.2 %copy-done = f32[2048,128]{1,0:T(8,128)S(1)} copy-done((f32[2048,128]{1,0:T(8,128)S(1)}, f32[2048,128]{1,0:T(8,128)}, u32[]{:S(2)}) %copy-start) | copy-done | bytes 1048600
  3.0 0.0 copy-start.1
  3.0 1.2 %copy-done.1 = f32[2048,128]{1,0:T(8,128)S(1)} copy-done((f32[2048,128]{1,0:T(8,128)S(1)}, f32[2048,128]{1,0:T(8,128)}, u32[]{:S(2)}) %copy-start.1) | copy-done | bytes 1048600
  4.2 0.0 copy-start.2
  4.2 1.0 %copy-done.2 = bf16[4,32,2048]{2,1,0:T(8,128)(2,1)S(1)} copy-done((bf16[4,32,2048]{2,1,0:T(8,128)(2,1)S(1)}, bf16[4,32,2048]{2,1,0:T(8,128)(2,1)}, u32[]{:S(2)}) %copy-start.2) | copy-done | bytes 524312
  5.2 0.0 copy-start.3
  5.3 1.0 %copy-done.3 = bf16[4,32,2048]{2,1,0:T(8,128)(2,1)S(1)} copy-done((bf16[4,32,2048]{2,1,0:T(8,128)(2,1)S(1)}, bf16[4,32,2048]{2,1,0:T(8,128)(2,1)}, u32[]{:S(2)}) %copy-start.3) | copy-done | bytes 524312
  6.3 0.0 copy-start.4
  6.3 0.7 %copy-done.4 = f32[2048]{0:T(1024)S(1)} copy-done((f32[2048]{0:T(1024)S(1)}, f32[2048]{0:T(1024)}, u32[]{:S(2)}) %copy-start.4) | copy-done | bytes 8216
  7.0 0.0 copy-start.5
  7.0 0.7 %copy-done.5 = f32[2048]{0:T(1024)S(1)} copy-done((f32[2048]{0:T(1024)S(1)}, f32[2048]{0:T(1024)}, u32[]{:S(2)}) %copy-start.5) | copy-done | bytes 8216
  7.7 0.0 copy-start.6
  7.7 0.7 %copy-done.6 = f32[2048]{0:T(1024)S(1)} copy-done((f32[2048]{0:T(1024)S(1)}, f32[2048]{0:T(1024)}, u32[]{:S(2)}) %copy-start.6) | copy-done | bytes 8216
  8.4 0.0 copy-start.7
  8.4 0.7 %copy-done.7 = f32[2048]{0:T(1024)S(1)} copy-done((f32[2048]{0:T(1024)S(1)}, f32[2048]{0:T(1024)}, u32[]{:S(2)}) %copy-start.7) | copy-done | bytes 8216
  9.1 0.0 copy-start.8
  9.1 0.7 %copy-done.8 = f32[2048]{0:T(1024)S(1)} copy-done((f32[2048]{0:T(1024)S(1)}, f32[2048]{0:T(1024)}, u32[]{:S(2)}) %copy-start.8) | copy-done | bytes 8216
  9.8 39.2 %shard_map.130 = (f32[2048,128]{1,0:T(8,128)S(1)}, f32[2048,128]{1,0:T(8,128)S(1)}, f32[1,128]{1,0:T(1,128)S(1)}) custom-call(s32[208]{0:T(256)S(1)} %add.81.index_ref, f32[2048,128]{1,0:T(8,128)S(1)} %copy-done, f32[2048,128]{1,0:T(8,128)S(1)} %copy-done.1, bf16[192,128,128]{2,1,0:T(8,128)(2,1)} %bitcast.17, bf16[128,2048]{1,0:T(8,128)(2,1)S(1)} %bitcast.9, ...), custom_call_target="tpu_custom_call" | custom-call | tf_op jit(solution)/shard_map/pallas_call | solution.py:418
  49.0 1.0 %copy.18 = f32[2048,128]{1,0:T(8,128)} copy(f32[2048,128]{1,0:T(8,128)S(1)} %get-tuple-element.12) | data formatting | bytes 2097152
  50.0 1.0 %copy.19 = f32[2048,128]{1,0:T(8,128)} copy(f32[2048,128]{1,0:T(8,128)S(1)} %get-tuple-element.13) | data formatting | bytes 2097152
  51.0 0.5 copy.20
  (4 shorter events, 0.0 us)
Async XLA Ops:
  1.8 1.2 %copy-start = (f32[2048,128]{1,0:T(8,128)S(1)}, f32[2048,128]{1,0:T(8,128)}, u32[]{:S(2)}) copy-start(f32[2048,128]{1,0:T(8,128)} %log_rate.1) | copy-start | bytes 3145732
  3.0 1.2 %copy-start.1 = (f32[2048,128]{1,0:T(8,128)S(1)}, f32[2048,128]{1,0:T(8,128)}, u32[]{:S(2)}) copy-start(f32[2048,128]{1,0:T(8,128)} %log_state.1) | copy-start | bytes 3145732
  4.2 1.0 %copy-start.2 = (bf16[4,32,2048]{2,1,0:T(8,128)(2,1)S(1)}, bf16[4,32,2048]{2,1,0:T(8,128)(2,1)}, u32[]{:S(2)}) copy-start(bf16[4,32,2048]{2,1,0:T(8,128)(2,1)} %param.15) | copy-start | bytes 1572868
  5.2 1.0 %copy-start.3 = (bf16[4,32,2048]{2,1,0:T(8,128)(2,1)S(1)}, bf16[4,32,2048]{2,1,0:T(8,128)(2,1)}, u32[]{:S(2)}) copy-start(bf16[4,32,2048]{2,1,0:T(8,128)(2,1)} %param.16) | copy-start | bytes 1572868
  6.3 0.7 %copy-start.4 = (f32[2048]{0:T(1024)S(1)}, f32[2048]{0:T(1024)}, u32[]{:S(2)}) copy-start(f32[2048]{0:T(1024)} %param.17) | copy-start | bytes 24580
  7.0 0.7 %copy-start.5 = (f32[2048]{0:T(1024)S(1)}, f32[2048]{0:T(1024)}, u32[]{:S(2)}) copy-start(f32[2048]{0:T(1024)} %param.18) | copy-start | bytes 24580
  7.7 0.7 %copy-start.6 = (f32[2048]{0:T(1024)S(1)}, f32[2048]{0:T(1024)}, u32[]{:S(2)}) copy-start(f32[2048]{0:T(1024)} %param.19) | copy-start | bytes 24580
  8.4 0.7 %copy-start.7 = (f32[2048]{0:T(1024)S(1)}, f32[2048]{0:T(1024)}, u32[]{:S(2)}) copy-start(f32[2048]{0:T(1024)} %param.20) | copy-start | bytes 24580
  9.1 0.7 %copy-start.8 = (f32[2048]{0:T(1024)S(1)}, f32[2048]{0:T(1024)}, u32[]{:S(2)}) copy-start(f32[2048]{0:T(1024)} %param.21) | copy-start | bytes 24580
